TPU v7x, 512 devices: a whole 4x8x8 slice. The times are simulated.
512 devices in a mesh: narrow: 16 (over x, y_lo), wide: 32 (over y_hi, z, core).
Axes of the slice: x: 4, y: 8 (y_hi: 2, y_lo: 4; y = y_hi * 4 + y_lo), z: 8, core: 2. Of those that a mesh axis runs over, the one named last changes fastest.
Arguments:
- out_grads: bfloat16 [512, 28672], P('wide', 'narrow'), may hold values from -0.5 to 0.5
- activations: bfloat16 [512, 8192], P('narrow', 'wide'), may hold values from -6 to 6
- grad_basis: bfloat16 [28672, 28672], P('narrow', 'wide'), may hold values from -0.03125 to 0.03125
- act_basis: bfloat16 [8192, 8192], P('wide', 'narrow'), may hold values from -0.0625 to 0.0625
Outputs:
- correction: bfloat16 [8192, 28672], P('narrow', 'wide')
All inputs are finite; a program needn't handle non-finite values.
Results may differ from a plain program's by a relative error of at most 0.0058.
Values may be sent and summed in bfloat16 or wider, within the bound.
No kernel may reach another device: no remote copies, remote signals or barrier semaphores. Data moves between devices by JAX's collectives and lax.ppermute only.
A program may use at most 64 MiB of HBM per device.

v0:
```python
import jax
import jax.numpy as jnp
from jax import lax
from jax.sharding import PartitionSpec as P

SEQ_LEN = 256


def shards(out_grads, activations, grad_basis, act_basis):
    grads_all = lax.all_gather(out_grads, "wide", axis=0, tiled=True)
    token_count = grads_all.shape[0]
    grad_part = jnp.dot(grads_all, grad_basis, preferred_element_type=jnp.float32)
    grad_rot = lax.psum(grad_part, "narrow").astype(jnp.bfloat16)
    acts_all = lax.all_gather(activations, "narrow", axis=0, tiled=True)
    act_part = jnp.dot(acts_all, act_basis, preferred_element_type=jnp.float32)
    act_rot = lax.psum(act_part, "wide").astype(jnp.bfloat16)
    seq_count = token_count // SEQ_LEN
    act_seq = act_rot.reshape(seq_count, SEQ_LEN, act_rot.shape[1])
    grad_seq = grad_rot.reshape(seq_count, SEQ_LEN, grad_rot.shape[1])
    products = jnp.einsum("sti,stj->sij", act_seq, grad_seq, preferred_element_type=jnp.float32)
    return jnp.mean(products * products, axis=0).astype(jnp.bfloat16)


def solution(mesh):
    return jax.shard_map(
        shards,
        mesh=mesh,
        in_specs=(
            P("wide", "narrow"),
            P("narrow", "wide"),
            P("narrow", "wide"),
            P("wide", "narrow"),
        ),
        out_specs=P("narrow", "wide"),
        check_vma=False,
    )
```

profile of v0, /device:TPU:22, one launch (start us, length us, event | category | flops | bytes accessed | tf_op | source)
XLA Modules:
  0.0 355.5 jit_solution(10772933344086978335)
XLA Ops:
  6.5 0.0 copy-start
  6.5 0.0 all-gather.2.cloned.1.call-start
  6.5 0.7 all-gather.2.cloned.1.call-update
  7.3 40.0 %all_gather.6 = bf16[512,256]{1,0:T(8,128)(2,1)S(1)} all-gather(bf16[32,256]{1,0:T(8,128)(2,1)} %param.5), channel_id=1, replica_groups=mesh['narrow'=16,'wide'=32] {'narrow'}, dimensions={0}, use_global_device_ids=true | all-gather | bytes 278528 | tf_op jit(solution)/shard_map/all_gather | solution.py:14
  47.3 2.2 fusion
  49.5 183.9 %all-reduce.3 = bf16[512,512]{1,0:T(8,128)(2,1)} all-reduce(f32[512,512]{1,0:T(8,128)} %fusion), channel_id=1, replica_groups=mesh['narrow'=16,'wide'=32] {'wide'}, use_global_device_ids=true, to_apply=%region_0.0 | all-reduce | flops 262144 | bytes 1572864 | tf_op jit(solution)/shard_map/psum | solution.py:16
  233.4 0.0 all-gather.2.cloned.1.call-done
  233.4 0.0 copy-done
  233.4 4.8 %fusion.1 = f32[512,896]{1,0:T(8,128)} fusion(bf16[512,1792]{1,0:T(8,128)(2,1)} %all-gather.2.cloned.1.call-done, bf16[1792,896]{1,0:T(8,128)(2,1)S(1)} %copy-done), kind=kOutput, calls=%fused_computation.3 | convolution fusion | flops 1644167168 | bytes 6881280 | tf_op jit(solution)/shard_map/dot_general | solution.py:12
  238.2 107.2 %all-reduce.2 = bf16[512,896]{1,0:T(8,128)(2,1)} all-reduce(f32[512,896]{1,0:T(8,128)} %fusion.1), channel_id=1, replica_groups=mesh['narrow'=16,'wide'=32] {'narrow'}, use_global_device_ids=true, to_apply=%region_1.0 | all-reduce | flops 458752 | bytes 2752512 | tf_op jit(solution)/shard_map/psum | solution.py:13
  345.4 2.3 multiply_reduce_fusion
  347.7 1.0 multiply_convert_fusion
Async XLA Ops:
  6.5 226.9 %copy-start = (bf16[1792,896]{1,0:T(8,128)(2,1)S(1)}, bf16[1792,896]{1,0:T(8,128)(2,1)}, u32[]{:S(2)}) copy-start(bf16[1792,896]{1,0:T(8,128)(2,1)} %param.6) | copy-start | bytes 9633796
  6.5 226.9 %all-gather.2.cloned.1.call-start = ((), (), s32[]{:S(2)}) async-start(), calls=%async_computation | async-start | bytes 1892352 | tf_op jit(solution)/shard_map/all_gather | solution.py:10
Sparse Core Ops, SparseCore 0:
  10.7 94.9 all-gather.1
where the time goes:
time: 356 us
  blocking collectives  331 us (93%)
  between operations  13.4 us (4%)
  matrix products  9.3 us (3%)
    psum x1, blocking collectives, shards(): act_rot = lax.psum(act_part, 'wide').astype(jnp.bfloat16)  184 us
    psum x1, blocking collectives, shards(): grad_rot = lax.psum(grad_part, 'narrow').astype(jnp.bfloat16)  107 us
    all_gather x1, blocking collectives, shards(): acts_all = lax.all_gather(activations, 'narrow', axis=0, tiled=True)  40 us
  transfers between devices with their start and end apart: 1, of which 0 were waited for; matrix products, arithmetic and copies ran while one was open for 1% of the time, Pallas kernels for 0%

commit v1 on v0

v1 whole, which is shorter than its diff:
```python
import jax
import jax.numpy as jnp
from jax import lax
from jax.experimental import pallas as pl
from jax.experimental.pallas import tpu as pltpu
from jax.sharding import Mesh, PartitionSpec as P

F32 = jnp.float32
BF16 = jnp.bfloat16
SEQS = 2
NARROW = ("x", "y_lo")
PLANE = ("y_hi", "z")
WIDE = PLANE + ("core",)
SIZES = (4, 4, 2, 8, 2)
PAIR = [(0, 1), (1, 0)]
VMEM = 40 * 2**20


def call(body, outs, *args, flops=0):
    moved = sum(a.size * a.dtype.itemsize for a in args)
    return pl.pallas_call(
        body,
        out_shape=outs,
        compiler_params=pltpu.CompilerParams(vmem_limit_bytes=VMEM),
        cost_estimate=pl.CostEstimate(flops=flops, bytes_accessed=moved, transcendentals=0),
    )(*args)


def spread(copies, axes):
    return lax.all_to_all(copies, axes, 0, 0)


def act_product(acts_ref, basis_ref, keep_ref, send_ref):
    core = lax.axis_index("core")
    for ref, part in ((keep_ref, core), (send_ref, 1 - core)):
        rows = acts_ref[:, pl.ds(part, 1)]
        rows = rows.reshape(ref.shape[0], basis_ref.shape[0])
        ref[...] = jnp.dot(rows, basis_ref[...], preferred_element_type=F32)


def add_pair(keep_ref, recv_ref, out_ref):
    out_ref[...] = (keep_ref[...] + recv_ref[...]).astype(BF16).reshape(out_ref.shape)


def add_and_copy(parts_ref, out_ref):
    total = parts_ref[0].astype(F32)
    for i in range(1, parts_ref.shape[0]):
        total = total + parts_ref[i].astype(F32)
    total = total.astype(BF16)
    for i in range(out_ref.shape[0]):
        out_ref[i] = total


def grad_product(own_ref, other_ref, basis_ref, out_ref):
    count, _, rows, width = out_ref.shape
    for which, ref in enumerate((own_ref, other_ref)):
        block = ref[...].reshape(count * rows, basis_ref.shape[0])
        part = jnp.dot(block, basis_ref[...], preferred_element_type=F32)
        out_ref[:, which] = part.astype(BF16).reshape(count, rows, width)


def correct(own_ref, other_ref, grad_ref, out_ref):
    count = grad_ref.shape[0] // SEQS
    total = None
    for seq in range(SEQS):
        part = slice(seq * count, (seq + 1) * count)
        acts = jnp.stack([own_ref[part], other_ref[part]], axis=1)
        acts = acts.reshape(-1, acts.shape[-1])
        grads = grad_ref[part].reshape(-1, grad_ref.shape[-1])
        product = lax.dot_general(acts, grads, (((0,), (0,)), ((), ())), preferred_element_type=F32)
        square = product * product
        total = square if total is None else total + square
    out_ref[...] = (total * (1.0 / SEQS)).astype(BF16)


def shards(out_grads, activations, grad_basis, act_basis):
    rows, depth = out_grads.shape
    acts_in = activations.shape[1]
    acts_out = act_basis.shape[1]
    width = grad_basis.shape[1]
    shape = jax.ShapeDtypeStruct

    grads = spread(jnp.broadcast_to(out_grads, (16, rows, depth)), PLANE)
    grads_other = lax.ppermute(grads, "core", PAIR)

    acts = activations.reshape(1, 2, rows, acts_in)
    acts = spread(jnp.broadcast_to(acts, (16, 2, rows, acts_in)), NARROW)
    half = shape((16 * rows, acts_out), F32)
    keep, send = call(act_product, (half, half), acts, act_basis)
    recv = lax.ppermute(send, "core", PAIR)
    act_half = call(add_pair, shape((16, rows, acts_out), BF16), keep, recv)
    act_parts = spread(act_half, PLANE)
    act_rot = call(add_and_copy, shape((16, rows, acts_out), BF16), act_parts)
    act_own = spread(act_rot, PLANE)
    act_other = lax.ppermute(act_own, "core", PAIR)

    grad_part = call(grad_product, shape((16, 2, rows, width), BF16), grads, grads_other, grad_basis)
    grad_parts = spread(grad_part, NARROW)
    grad_rot = call(add_and_copy, shape((4, 2, rows, width), BF16), grad_parts)
    grad_rot = spread(grad_rot, "y_lo")
    grad_rot = lax.all_gather(grad_rot, "x", axis=0, tiled=True)

    return call(correct, shape((acts_out, width), BF16), act_own, act_other, grad_rot)


def solution(mesh):
    fine = Mesh(mesh.devices.reshape(SIZES), NARROW + WIDE)
    return jax.shard_map(
        shards,
        mesh=fine,
        in_specs=(
            P(WIDE, NARROW),
            P(NARROW, WIDE),
            P(NARROW, WIDE),
            P(WIDE, NARROW),
        ),
        out_specs=P(NARROW, WIDE),
        check_vma=False,
    )
```

time: 356 us -> 159 us (0.45)
  the two profiles are of different devices: /device:TPU:22 before, /device:TPU:8 now
where the time goes in v1:
time: 159 us; the launch traced here: 158 us
  waiting for transfers between devices  72.8 us (46%)
  starting transfers between devices  41.3 us (26%)
  blocking collectives  30.9 us (19%)
  Pallas kernels  8.1 us (5%)
  local copies, waits for them, and re-layouts  4.48 us (3%)
    all_to_all x5, waiting for transfers between devices, spread(): return lax.all_to_all(copies, axes, 0, 0)  72.8 us
    all_to_all x5, starting transfers between devices, spread(): return lax.all_to_all(copies, axes, 0, 0)  35.6 us
    all_to_all x1, blocking collectives, spread(): return lax.all_to_all(copies, axes, 0, 0)  16.8 us
    all_gather x1, blocking collectives, shards(): grad_rot = lax.all_gather(grad_rot, 'x', axis=0, tiled=True)  14.1 us
    pallas_call x6, Pallas kernels, call(): pl.pallas_call(body, out_shape=outs, compiler_params=pltpu.CompilerParams...  8.1 us
  transfers between devices with their start and end apart: 8, of which 5 were waited for; matrix products, arithmetic and copies ran while one was open for 0% of the time, Pallas kernels for 4%

profile of v1, /device:TPU:8, one launch (start us, length us, event | category | flops | bytes accessed | tf_op | source)
XLA Modules:
  0.0 157.8 jit_solution(7307184207660048782)
XLA Ops:
  0.0 0.8 broadcast_in_dim.11
  0.8 16.8 %all_to_all.30.acts_ref = bf16[16,2,16,256]{3,2,1,0:T(8,128)(2,1)S(1)} all-to-all(bf16[16,2,16,256]{3,2,1,0:T(8,128)(2,1)S(1)} %broadcast_in_dim.11), channel_id=1, replica_groups=mesh['x'=4,'y_lo'=4,'y_hi'=2,'z'=8,'core'=2] {'x','y_lo'}, dimensions={0} | all-to-all | bytes 524288 | tf_op jit(solution)/shard_map/all_to_all | solution.py:30
  17.6 1.8 %broadcast_in_dim.12 = bf16[16,16,1792]{2,1,0:T(8,128)(2,1)} broadcast(bf16[16,1792]{1,0:T(8,128)(2,1)} %param.4), dimensions={1,2} | broadcast | bytes 974848 | tf_op jit(solution)/shard_map/broadcast_in_dim | solution.py:83
  19.4 13.0 %all-to-all-start.3 = ((bf16[16,16,1792]{2,1,0:T(8,128)(2,1)}), bf16[16,16,1792]{2,1,0:T(8,128)(2,1)S(1)}, u32[]{:S(2)}, u32[]{:S(2)}) async-start(bf16[16,16,1792]{2,1,0:T(8,128)(2,1)} %broadcast_in_dim.12), calls=%async_computation.3 | async-start | bytes 1835008 | tf_op jit(solution)/shard_map/all_to_all | solution.py:30
  32.4 1.1 shard_map.46
  33.4 1.9 %collective-permute-start = (f32[256,512]{1,0:T(8,128)}, f32[256,512]{1,0:T(8,128)S(1)}, u32[]{:S(2)}, u32[]{:S(2)}) collective-permute-start(f32[256,512]{1,0:T(8,128)} %get-tuple-element.8), channel_id=1, source_target_pairs={{0,1},{1,0},{2,3},{3,2},{4,5},{5,4},{6,7},{7,6},{8,9},{9,8},{10,11... | collective-permute-start | bytes 1572872 | tf_op jit(solution)/shard_map/ppermute | solution.py:90
  35.4 25.6 %all-to-all-done.3.own_ref = bf16[16,16,1792]{2,1,0:T(8,128)(2,1)S(1)} async-done(((bf16[16,16,1792]{2,1,0:T(8,128)(2,1)}), bf16[16,16,1792]{2,1,0:T(8,128)(2,1)S(1)}, u32[]{:S(2)}, u32[]{:S(2)}) %all-to-all-start.3) | async-done | bytes 917536 | tf_op jit(solution)/shard_map/all_to_all | solution.py:30
  61.0 1.9 %collective-permute-start.2 = (bf16[16,16,1792]{2,1,0:T(8,128)(2,1)S(1)}, bf16[16,16,1792]{2,1,0:T(8,128)(2,1)S(1)}, u32[]{:S(2)}, u32[]{:S(2)}) collective-permute-start(bf16[16,16,1792]{2,1,0:T(8,128)(2,1)S(1)} %all-to-all-done.3.own_ref), channel_id=1, source_target_pairs={{0,1},{1,0},{2,3},{3,2},{4,5},{5,4},{6,7},{7,6},{8,9},{9,8},{10,11... | collective-permute-start | bytes 2752520 | tf_op jit(solution)/shard_map/ppermute | solution.py:84
  62.9 0.7 shard_map.47
  63.6 5.9 %all-to-all-start.1 = ((bf16[16,16,512]{2,1,0:T(8,128)(2,1)}), bf16[16,16,512]{2,1,0:T(8,128)(2,1)S(1)}, u32[]{:S(2)}, u32[]{:S(2)}) async-start(bf16[16,16,512]{2,1,0:T(8,128)(2,1)} %shard_map.47), calls=%async_computation.1 | async-start | bytes 524288 | tf_op jit(solution)/shard_map/all_to_all | solution.py:30
  69.6 1.9 %copy-done = bf16[1792,896]{1,0:T(8,128)(2,1)S(1)} copy-done((bf16[1792,896]{1,0:T(8,128)(2,1)S(1)}, bf16[1792,896]{1,0:T(8,128)(2,1)}, u32[]{:S(2)}) %copy-start) | copy-done | bytes 3211288
  71.5 3.0 %shard_map.49 = bf16[16,2,16,896]{3,2,1,0:T(8,128)(2,1)} custom-call(bf16[16,16,1792]{2,1,0:T(8,128)(2,1)S(1)} %all-to-all-done.3.own_ref, bf16[16,16,1792]{2,1,0:T(8,128)(2,1)S(1)} %collective-permute-done.2.other_ref, bf16[1792,896]{1,0:T(8,128)(2,1)S(1)} %copy-done), custom_call_target="tpu_custom_call" | custom-call | bytes 5046272 | tf_op jit(solution)/shard_map/pallas_call | solution.py:21
  74.5 9.0 %all-to-all-done.1.parts_ref = bf16[16,16,512]{2,1,0:T(8,128)(2,1)S(1)} async-done(((bf16[16,16,512]{2,1,0:T(8,128)(2,1)}), bf16[16,16,512]{2,1,0:T(8,128)(2,1)S(1)}, u32[]{:S(2)}, u32[]{:S(2)}) %all-to-all-start.1) | async-done | bytes 262176 | tf_op jit(solution)/shard_map/all_to_all | solution.py:30
  83.5 5.6 %all-to-all-start.4 = ((bf16[16,2,16,896]{3,2,1,0:T(8,128)(2,1)}), bf16[16,2,16,896]{3,2,1,0:T(8,128)(2,1)S(1)}, u32[]{:S(2)}, u32[]{:S(2)}) async-start(bf16[16,2,16,896]{3,2,1,0:T(8,128)(2,1)} %shard_map.49), calls=%async_computation.4 | async-start | bytes 1835008 | tf_op jit(solution)/shard_map/all_to_all | solution.py:30
  89.1 0.8 shard_map.48
  89.8 20.4 %all-to-all-done.4.parts_ref = bf16[16,2,16,896]{3,2,1,0:T(8,128)(2,1)S(1)} async-done(((bf16[16,2,16,896]{3,2,1,0:T(8,128)(2,1)}), bf16[16,2,16,896]{3,2,1,0:T(8,128)(2,1)S(1)}, u32[]{:S(2)}, u32[]{:S(2)}) %all-to-all-start.4) | async-done | bytes 917536 | tf_op jit(solution)/shard_map/all_to_all | solution.py:30
  110.3 5.9 %all-to-all-start.2 = ((bf16[16,16,512]{2,1,0:T(8,128)(2,1)}), bf16[16,16,512]{2,1,0:T(8,128)(2,1)S(1)}, u32[]{:S(2)}, u32[]{:S(2)}) async-start(bf16[16,16,512]{2,1,0:T(8,128)(2,1)} %shard_map.48), calls=%async_computation.2 | async-start | bytes 524288 | tf_op jit(solution)/shard_map/all_to_all | solution.py:30
  116.2 0.8 shard_map.50
  117.0 13.7 %all-to-all-done.2.own_ref = bf16[16,16,512]{2,1,0:T(8,128)(2,1)S(1)} async-done(((bf16[16,16,512]{2,1,0:T(8,128)(2,1)}), bf16[16,16,512]{2,1,0:T(8,128)(2,1)S(1)}, u32[]{:S(2)}, u32[]{:S(2)}) %all-to-all-start.2) | async-done | bytes 262176 | tf_op jit(solution)/shard_map/all_to_all | solution.py:30
  130.8 5.2 %all-to-all-start.5 = ((bf16[4,2,16,896]{3,2,1,0:T(8,128)(2,1)}), bf16[4,2,16,896]{3,2,1,0:T(8,128)(2,1)S(1)}, u32[]{:S(2)}, u32[]{:S(2)}) async-start(bf16[4,2,16,896]{3,2,1,0:T(8,128)(2,1)} %shard_map.50), calls=%async_computation.5 | async-start | bytes 458752 | tf_op jit(solution)/shard_map/all_to_all | solution.py:30
  136.0 1.9 %collective-permute-start.1 = (bf16[16,16,512]{2,1,0:T(8,128)(2,1)S(1)}, bf16[16,16,512]{2,1,0:T(8,128)(2,1)S(1)}, u32[]{:S(2)}, u32[]{:S(2)}) collective-permute-start(bf16[16,16,512]{2,1,0:T(8,128)(2,1)S(1)} %all-to-all-done.2.own_ref), channel_id=1, source_target_pairs={{0,1},{1,0},{2,3},{3,2},{4,5},{5,4},{6,7},{7,6},{8,9},{9,8},{10,11... | collective-permute-start | bytes 786440 | tf_op jit(solution)/shard_map/ppermute | solution.py:95
  137.9 4.0 %all-to-all-done.5 = bf16[4,2,16,896]{3,2,1,0:T(8,128)(2,1)S(1)} async-done(((bf16[4,2,16,896]{3,2,1,0:T(8,128)(2,1)}), bf16[4,2,16,896]{3,2,1,0:T(8,128)(2,1)S(1)}, u32[]{:S(2)}, u32[]{:S(2)}) %all-to-all-start.5) | async-done | bytes 229408 | tf_op jit(solution)/shard_map/all_to_all | solution.py:30
  141.9 14.1 %all_gather.3.grad_ref = bf16[16,2,16,896]{3,2,1,0:T(8,128)(2,1)S(1)} all-gather(bf16[4,2,16,896]{3,2,1,0:T(8,128)(2,1)S(1)} %all-to-all-done.5), channel_id=1, replica_groups=mesh['x'=4,'y_lo'=4,'y_hi'=2,'z'=8,'core'=2] {'x'}, dimensions={0}, use_global_device_ids=true | all-gather | bytes 1146880 | tf_op jit(solution)/shard_map/all_gather | solution.py:101
  156.1 1.7 %shard_map.51 = bf16[512,896]{1,0:T(8,128)(2,1)} custom-call(bf16[16,16,512]{2,1,0:T(8,128)(2,1)S(1)} %all-to-all-done.2.own_ref, bf16[16,16,512]{2,1,0:T(8,128)(2,1)S(1)} %collective-permute-done.1.other_ref, bf16[16,2,16,896]{3,2,1,0:T(8,128)(2,1)S(1)} %all_gather.3.grad_ref), custom_call_target="tpu_custom_call" | custom-call | bytes 1441792 | tf_op jit(solution)/shard_map/pallas_call | solution.py:21
  (6 shorter events, 0.0 us)
Async XLA Ops:
  0.0 32.3 %copy-start.1 = (bf16[256,512]{1,0:T(8,128)(2,1)S(1)}, bf16[256,512]{1,0:T(8,128)(2,1)}, u32[]{:S(2)}) copy-start(bf16[256,512]{1,0:T(8,128)(2,1)} %basis_ref.2) | copy-start | bytes 786436
  19.4 41.6 %all-to-all-start.3 = ((bf16[16,16,1792]{2,1,0:T(8,128)(2,1)}), bf16[16,16,1792]{2,1,0:T(8,128)(2,1)S(1)}, u32[]{:S(2)}, u32[]{:S(2)}) async-start(bf16[16,16,1792]{2,1,0:T(8,128)(2,1)} %broadcast_in_dim.12), calls=%async_computation.3 | async-start | bytes 1835008 | tf_op jit(solution)/shard_map/all_to_all | solution.py:30
  33.4 29.4 %collective-permute-start = (f32[256,512]{1,0:T(8,128)}, f32[256,512]{1,0:T(8,128)S(1)}, u32[]{:S(2)}, u32[]{:S(2)}) collective-permute-start(f32[256,512]{1,0:T(8,128)} %get-tuple-element.8), channel_id=1, source_target_pairs={{0,1},{1,0},{2,3},{3,2},{4,5},{5,4},{6,7},{7,6},{8,9},{9,8},{10,11... | collective-permute-start | bytes 1572872 | tf_op jit(solution)/shard_map/ppermute | solution.py:90
  61.0 8.6 %collective-permute-start.2 = (bf16[16,16,1792]{2,1,0:T(8,128)(2,1)S(1)}, bf16[16,16,1792]{2,1,0:T(8,128)(2,1)S(1)}, u32[]{:S(2)}, u32[]{:S(2)}) collective-permute-start(bf16[16,16,1792]{2,1,0:T(8,128)(2,1)S(1)} %all-to-all-done.3.own_ref), channel_id=1, source_target_pairs={{0,1},{1,0},{2,3},{3,2},{4,5},{5,4},{6,7},{7,6},{8,9},{9,8},{10,11... | collective-permute-start | bytes 2752520 | tf_op jit(solution)/shard_map/ppermute | solution.py:84
  63.6 19.9 %all-to-all-start.1 = ((bf16[16,16,512]{2,1,0:T(8,128)(2,1)}), bf16[16,16,512]{2,1,0:T(8,128)(2,1)S(1)}, u32[]{:S(2)}, u32[]{:S(2)}) async-start(bf16[16,16,512]{2,1,0:T(8,128)(2,1)} %shard_map.47), calls=%async_computation.1 | async-start | bytes 524288 | tf_op jit(solution)/shard_map/all_to_all | solution.py:30
  69.6 1.9 %copy-start = (bf16[1792,896]{1,0:T(8,128)(2,1)S(1)}, bf16[1792,896]{1,0:T(8,128)(2,1)}, u32[]{:S(2)}) copy-start(bf16[1792,896]{1,0:T(8,128)(2,1)} %basis_ref.3) | copy-start | bytes 9633796
  83.5 26.7 %all-to-all-start.4 = ((bf16[16,2,16,896]{3,2,1,0:T(8,128)(2,1)}), bf16[16,2,16,896]{3,2,1,0:T(8,128)(2,1)S(1)}, u32[]{:S(2)}, u32[]{:S(2)}) async-start(bf16[16,2,16,896]{3,2,1,0:T(8,128)(2,1)} %shard_map.49), calls=%async_computation.4 | async-start | bytes 1835008 | tf_op jit(solution)/shard_map/all_to_all | solution.py:30
  110.3 20.5 %all-to-all-start.2 = ((bf16[16,16,512]{2,1,0:T(8,128)(2,1)}), bf16[16,16,512]{2,1,0:T(8,128)(2,1)S(1)}, u32[]{:S(2)}, u32[]{:S(2)}) async-start(bf16[16,16,512]{2,1,0:T(8,128)(2,1)} %shard_map.48), calls=%async_computation.2 | async-start | bytes 524288 | tf_op jit(solution)/shard_map/all_to_all | solution.py:30
  130.8 11.1 %all-to-all-start.5 = ((bf16[4,2,16,896]{3,2,1,0:T(8,128)(2,1)}), bf16[4,2,16,896]{3,2,1,0:T(8,128)(2,1)S(1)}, u32[]{:S(2)}, u32[]{:S(2)}) async-start(bf16[4,2,16,896]{3,2,1,0:T(8,128)(2,1)} %shard_map.50), calls=%async_computation.5 | async-start | bytes 458752 | tf_op jit(solution)/shard_map/all_to_all | solution.py:30
  136.0 20.1 %collective-permute-start.1 = (bf16[16,16,512]{2,1,0:T(8,128)(2,1)S(1)}, bf16[16,16,512]{2,1,0:T(8,128)(2,1)S(1)}, u32[]{:S(2)}, u32[]{:S(2)}) collective-permute-start(bf16[16,16,512]{2,1,0:T(8,128)(2,1)S(1)} %all-to-all-done.2.own_ref), channel_id=1, source_target_pairs={{0,1},{1,0},{2,3},{3,2},{4,5},{5,4},{6,7},{7,6},{8,9},{9,8},{10,11... | collective-permute-start | bytes 786440 | tf_op jit(solution)/shard_map/ppermute | solution.py:95

commit v2 on v1

v2 whole, which is shorter than its diff:
```python
import jax
import jax.numpy as jnp
from jax import lax
from jax.experimental import pallas as pl
from jax.experimental.pallas import tpu as pltpu
from jax.sharding import Mesh, PartitionSpec as P

F32 = jnp.float32
BF16 = jnp.bfloat16
SEQS = 2
NARROW = ("x", "y_lo")
PLANE = ("y_hi", "z")
WIDE = PLANE + ("core",)
SIZES = (4, 4, 2, 8, 2)
PAIR = [(0, 1), (1, 0)]
VMEM = 40 * 2**20
STEP = 896
shape = jax.ShapeDtypeStruct


def call(body, outs, *args, flops=0, **more):
    moved = sum(a.size * a.dtype.itemsize for a in args)
    return pl.pallas_call(
        body,
        out_shape=outs,
        compiler_params=pltpu.CompilerParams(vmem_limit_bytes=VMEM),
        cost_estimate=pl.CostEstimate(flops=flops, bytes_accessed=moved, transcendentals=0),
        **more,
    )(*args)


def spread(copies, axes):
    return lax.all_to_all(copies, axes, 0, 0)


def act_product(acts_ref, basis_ref, keep_ref, send_ref):
    core = lax.axis_index("core")
    for ref, part in ((keep_ref, core), (send_ref, 1 - core)):
        rows = acts_ref[:, pl.ds(part, 1)]
        rows = rows.reshape(ref.shape[0], basis_ref.shape[0])
        ref[...] = jnp.dot(rows, basis_ref[...], preferred_element_type=F32)


def pack(grads_ref, keep_ref, recv_ref, out_ref):
    count = out_ref.shape[0]
    half, rows, depth = grads_ref.shape
    for i in range(count):
        for j in range(half):
            part = slice((j * count + i) * rows, (j * count + i + 1) * rows)
            out_ref[i, j, :, :depth] = grads_ref[j]
            out_ref[i, j, :, depth:] = (keep_ref[part] + recv_ref[part]).astype(BF16)


def total_of(parts):
    total = parts[0].astype(F32)
    for i in range(1, parts.shape[0]):
        total = total + parts[i].astype(F32)
    return total


def add_acts(packed_ref, out_ref):
    out_ref[...] = total_of(packed_ref[:, :, :, packed_ref.shape[3] - out_ref.shape[2]:])


def add_far(own_ref, far_ref, out_ref):
    out_ref[...] = (own_ref[...] + far_ref[...]).astype(BF16)


def place(own_ref, other_ref, out_ref):
    here = lax.axis_index("y_hi")
    out_ref[pl.ds(here, 1)] = own_ref[...][None]
    out_ref[pl.ds(1 - here, 1)] = other_ref[...][None]


def add_grads(parts_ref, out_ref):
    total = total_of(parts_ref).astype(BF16)
    for i in range(out_ref.shape[0]):
        out_ref[i] = total


def own_product(own_ref, basis_ref, out_ref, sums_ref):
    step = pl.program_id(0)
    block = own_ref[...].reshape(sums_ref.shape[0], STEP)
    part = jnp.dot(block, basis_ref[...], preferred_element_type=F32)

    @pl.when(step == 0)
    def _():
        sums_ref[...] = part

    @pl.when(step == pl.num_programs(0) - 1)
    def _():
        out_ref[...] = (sums_ref[...] + part).astype(BF16)


def other_product(first_ref, other_ref, basis_ref, out_ref, sums_ref):
    step = pl.program_id(0)
    halves, count, _, rows, width = out_ref.shape
    block = other_ref[...].reshape(sums_ref.shape[0], STEP)
    part = jnp.dot(block, basis_ref[...], preferred_element_type=F32)

    @pl.when(step == 0)
    def _():
        sums_ref[...] = part
        first = first_ref[...].reshape(count, halves, rows, width)
        for j in range(halves):
            out_ref[j, :, 0] = first[:, j]

    @pl.when(step == pl.num_programs(0) - 1)
    def _():
        last = (sums_ref[...] + part).astype(BF16).reshape(count, halves, rows, width)
        for j in range(halves):
            out_ref[j, :, 1] = last[:, j]


def correct(own_ref, other_ref, grad_ref, out_ref):
    count = grad_ref.shape[0] // SEQS
    total = None
    for seq in range(SEQS):
        acts = jnp.stack([own_ref[:, seq], other_ref[:, seq]], axis=1)
        acts = acts.reshape(-1, acts.shape[-1])
        grads = grad_ref[seq * count:(seq + 1) * count]
        grads = grads.reshape(-1, grads.shape[-1])
        product = lax.dot_general(acts, grads, (((0,), (0,)), ((), ())), preferred_element_type=F32)
        square = product * product
        total = square if total is None else total + square
    out_ref[...] = (total * (1.0 / SEQS)).astype(BF16)


def shards(out_grads, activations, grad_basis, act_basis):
    rows, depth = out_grads.shape
    acts_in = activations.shape[1]
    acts_out = act_basis.shape[1]
    width = grad_basis.shape[1]

    acts = activations.reshape(1, 2, rows, acts_in)
    acts = spread(jnp.broadcast_to(acts, (16, 2, rows, acts_in)), NARROW)
    grads_far = lax.ppermute(out_grads, "y_hi", PAIR)
    grads = call(place, shape((2, rows, depth), BF16), out_grads, grads_far)
    acts, grads = lax.optimization_barrier((acts, grads))
    half = shape((16 * rows, acts_out), F32)
    keep, send = call(act_product, (half, half), acts, act_basis)
    recv = lax.ppermute(send, "core", PAIR)

    packed = call(pack, shape((8, 2, rows, depth + acts_out), BF16), grads, keep, recv)
    packed = spread(packed, "z")
    packed_other = lax.ppermute(packed, "core", PAIR)

    act_near = call(add_acts, shape((2, rows, acts_out), F32), packed)
    act_far = lax.ppermute(act_near, "y_hi", PAIR)

    specs = [
        pl.BlockSpec((8, 2, rows, STEP), lambda k: (0, 0, 0, k)),
        pl.BlockSpec((STEP, width), lambda k: (k, 0)),
    ]
    more = dict(grid=(depth // STEP,), scratch_shapes=[pltpu.VMEM((16 * rows, width), F32)])
    first = call(
        own_product,
        shape((16 * rows, width), BF16),
        packed,
        grad_basis,
        in_specs=specs,
        out_specs=pl.BlockSpec((16 * rows, width), lambda k: (0, 0)),
        **more,
    )
    grad_part = call(
        other_product,
        shape((2, 8, 2, rows, width), BF16),
        first,
        packed_other,
        grad_basis,
        in_specs=[pl.BlockSpec((16 * rows, width), lambda k: (0, 0))] + specs,
        out_specs=pl.BlockSpec((2, 8, 2, rows, width), lambda k: (0, 0, 0, 0, 0)),
        **more,
    )
    act_two = call(add_far, shape((2, rows, acts_out), BF16), act_near, act_far)
    grad_part, act_two = lax.optimization_barrier((grad_part, act_two))
    grad_parts = spread(grad_part.reshape(16, 2, rows, width), NARROW)
    act_own = lax.all_gather(act_two, "z", axis=0)
    grad_parts, act_own = lax.optimization_barrier((grad_parts, act_own))
    act_other = lax.ppermute(act_own, "core", PAIR)

    grad_rot = call(add_grads, shape((4, 2, rows, width), BF16), grad_parts)
    grad_rot = spread(grad_rot, "y_lo")
    grad_rot = lax.all_gather(grad_rot, "x", axis=0, tiled=True)
    return call(correct, shape((acts_out, width), BF16), act_own, act_other, grad_rot)


def solution(mesh):
    fine = Mesh(mesh.devices.reshape(SIZES), NARROW + WIDE)
    return jax.shard_map(
        shards,
        mesh=fine,
        in_specs=(
            P(WIDE, NARROW),
            P(NARROW, WIDE),
            P(NARROW, WIDE),
            P(WIDE, NARROW),
        ),
        out_specs=P(NARROW, WIDE),
        check_vma=False,
    )
```

time: 159 us -> 145 us (0.912)
  waiting for transfers between devices: 72.8 us -> 16.3 us
  blocking collectives: 30.9 us -> 81.3 us
  starting transfers between devices: 41.3 us -> 36.9 us
  local copies, waits for them, and re-layouts: 4.48 us -> 2.32 us
    all_to_all x5 -> x3, waiting for transfers between devices: 72.8 us -> 4.04 us  [spread(): return lax.all_to_all(copies, axes, 0, 0)]
    all_gather x0 -> x1, blocking collectives: none -> 24.9 us  [shards(): act_own = lax.all_gather(act_two, 'z', axis=0)]
    all_to_all x1, blocking collectives: 16.8 us -> 41.5 us  [spread(): return lax.all_to_all(copies, axes, 0, 0)]
    all_to_all x5 -> x3, starting transfers between devices: 35.6 us -> 22.6 us  [spread(): return lax.all_to_all(copies, axes, 0, 0)]
    ppermute x1 -> x3, waiting for transfers between devices: 0.01 us -> 10.4 us  [the longest x1 6.63 us: shards(): grads_far = lax.ppermute(out_grads, 'y_hi', PAIR)]
    ppermute x1 -> x3, starting transfers between devices: 1.91 us -> 10.5 us  [the longest x1 4.94 us: shards(): act_far = lax.ppermute(act_near, 'y_hi', PAIR)]
    ppermute x1, waiting for transfers between devices: 0.01 us -> 1.88 us  [shards(): recv = lax.ppermute(send, 'core', PAIR)]
    broadcast_in_dim x1 -> x0, local copies, waits for them, and re-layouts: 1.8 us -> none  [shards(): grads = spread(jnp.broadcast_to(out_grads, (16, rows, depth)), PLANE)]
  transfers between devices with their start and end apart: 8 -> 8, of which waited for: 5 -> 4; matrix products, arithmetic and copies ran while one was open for 0% -> 0% of each run, Pallas kernels for 4% -> 1%
where the time goes in v2:
time: 145 us; the launch traced here: 144 us
  blocking collectives  81.3 us (56%)
  starting transfers between devices  36.9 us (25%)
  waiting for transfers between devices  16.3 us (11%)
  Pallas kernels  7.29 us (5%)
  local copies, waits for them, and re-layouts  2.32 us (2%)
    all_to_all x1, blocking collectives, spread(): return lax.all_to_all(copies, axes, 0, 0)  41.5 us
    all_gather x1, blocking collectives, shards(): act_own = lax.all_gather(act_two, 'z', axis=0)  24.9 us
    all_to_all x3, starting transfers between devices, spread(): return lax.all_to_all(copies, axes, 0, 0)  22.6 us
    all_gather x1, blocking collectives, shards(): grad_rot = lax.all_gather(grad_rot, 'x', axis=0, tiled=True)  14.9 us
    pallas_call x9, Pallas kernels, call(): pl.pallas_call(body, out_shape=outs, compiler_params=pltpu.CompilerParams...  7.29 us
    ppermute x1, waiting for transfers between devices, shards(): grads_far = lax.ppermute(out_grads, 'y_hi', PAIR)  6.63 us
    ppermute x1, starting transfers between devices, shards(): act_far = lax.ppermute(act_near, 'y_hi', PAIR)  4.94 us
    all_to_all x3, waiting for transfers between devices, spread(): return lax.all_to_all(copies, axes, 0, 0)  4.04 us
  transfers between devices with their start and end apart: 8, of which 4 were waited for; matrix products, arithmetic and copies ran while one was open for 0% of the time, Pallas kernels for 1%

profile of v2, /device:TPU:8, one launch (start us, length us, event | category | flops | bytes accessed | tf_op | source)
XLA Modules:
  0.0 144.3 jit_solution(4647235074972871811)
XLA Ops:
  0.0 1.5 %broadcast_in_dim.8 = bf16[16,2,16,256]{3,2,1,0:T(8,128)(2,1)} broadcast(bf16[2,16,256]{2,1,0:T(8,128)(2,1)} %bitcast.5), dimensions={1,2,3} | broadcast | bytes 278528 | tf_op jit(solution)/shard_map/broadcast_in_dim | solution.py:136
  1.5 9.1 %all-to-all-start = ((bf16[16,2,16,256]{3,2,1,0:T(8,128)(2,1)}), bf16[16,2,16,256]{3,2,1,0:T(8,128)(2,1)S(1)}, u32[]{:S(2)}, u32[]{:S(2)}) async-start(bf16[16,2,16,256]{3,2,1,0:T(8,128)(2,1)} %broadcast_in_dim.8), calls=%async_computation | async-start | bytes 524288 | tf_op jit(solution)/shard_map/all_to_all | solution.py:33
  10.6 3.7 %collective-permute-start = (bf16[16,1792]{1,0:T(8,128)(2,1)}, bf16[16,1792]{1,0:T(8,128)(2,1)S(1)}, u32[]{:S(2)}, u32[]{:S(2)}) collective-permute-start(bf16[16,1792]{1,0:T(8,128)(2,1)} %own_ref.1), channel_id=1, source_target_pairs={{0,16},{16,0},{1,17},{17,1},{2,18},{18,2},{3,19},{19,3},{4,20},{20... | collective-permute-start | bytes 172040 | tf_op jit(solution)/shard_map/ppermute | solution.py:137
  14.3 6.6 %collective-permute-done.other_ref = bf16[16,1792]{1,0:T(8,128)(2,1)S(1)} collective-permute-done((bf16[16,1792]{1,0:T(8,128)(2,1)}, bf16[16,1792]{1,0:T(8,128)(2,1)S(1)}, u32[]{:S(2)}, u32[]{:S(2)}) %collective-permute-start) | collective-permute-done | bytes 57376 | tf_op jit(solution)/shard_map/ppermute | solution.py:137
  21.0 0.8 copy-done.2
  21.8 0.3 shard_map.47
  22.1 1.9 %collective-permute-start.1 = (f32[256,512]{1,0:T(8,128)S(1)}, f32[256,512]{1,0:T(8,128)S(1)}, u32[]{:S(2)}, u32[]{:S(2)}) collective-permute-start(f32[256,512]{1,0:T(8,128)S(1)} %get-tuple-element.16), channel_id=1, source_target_pairs={{0,1},{1,0},{2,3},{3,2},{4,5},{5,4},{6,7},{7,6},{8,9},{9,8},{10,11... | collective-permute-start | bytes 1572872 | tf_op jit(solution)/shard_map/ppermute | solution.py:142
  24.0 1.9 %collective-permute-done.1.recv_ref = f32[256,512]{1,0:T(8,128)S(1)} collective-permute-done((f32[256,512]{1,0:T(8,128)S(1)}, f32[256,512]{1,0:T(8,128)S(1)}, u32[]{:S(2)}, u32[]{:S(2)}) %collective-permute-start.1) | collective-permute-done | bytes 524320 | tf_op jit(solution)/shard_map/ppermute | solution.py:142
  25.9 0.1 shard_map.48
  26.0 0.0 copy-start
  26.0 41.5 %all_to_all.20.own_ref.packed_ref = bf16[8,2,16,2304]{3,2,1,0:T(8,128)(2,1)S(1)} all-to-all(bf16[8,2,16,2304]{3,2,1,0:T(8,128)(2,1)S(1)} %shard_map.48), channel_id=1, replica_groups=mesh['x'=4,'y_lo'=4,'y_hi'=2,'z'=8,'core'=2] {'z'}, dimensions={0} | all-to-all | bytes 2359296 | tf_op jit(solution)/shard_map/all_to_all | solution.py:33
  67.5 1.9 %collective-permute-start.2 = (bf16[8,2,16,2304]{3,2,1,0:T(8,128)(2,1)S(1)}, bf16[8,2,16,2304]{3,2,1,0:T(8,128)(2,1)S(1)}, u32[]{:S(2)}, u32[]{:S(2)}) collective-permute-start(bf16[8,2,16,2304]{3,2,1,0:T(8,128)(2,1)S(1)} %all_to_all.20.own_ref.packed_ref), channel_id=1, source_target_pairs={{0,1},{1,0},{2,3},{3,2},{4,5},{5,4},{6,7},{7,6},{8,9},{9,8},{10,11... | collective-permute-start | bytes 3538952 | tf_op jit(solution)/shard_map/ppermute | solution.py:146
  69.5 4.9 %collective-permute-start.3 = (f32[2,16,512]{2,1,0:T(8,128)S(1)}, f32[2,16,512]{2,1,0:T(8,128)S(1)}, u32[]{:S(2)}, u32[]{:S(2)}) collective-permute-start(f32[2,16,512]{2,1,0:T(8,128)S(1)} %shard_map.51.own_ref), channel_id=1, source_target_pairs={{0,16},{16,0},{1,17},{17,1},{2,18},{18,2},{3,19},{19,3},{4,20},{20... | collective-permute-start | bytes 196616 | tf_op jit(solution)/shard_map/ppermute | solution.py:149
  74.5 1.7 %shard_map.49.first_ref = bf16[256,896]{1,0:T(8,128)(2,1)S(1)} custom-call(bf16[8,2,16,2304]{3,2,1,0:T(8,128)(2,1)S(1)} %all_to_all.20.own_ref.packed_ref, bf16[1792,896]{1,0:T(8,128)(2,1)S(1)} %copy-done), custom_call_target="tpu_custom_call" | custom-call | bytes 4390912 | tf_op jit(solution)/shard_map/pallas_call | solution.py:23
  76.2 3.7 %collective-permute-done.3.far_ref = f32[2,16,512]{2,1,0:T(8,128)S(1)} collective-permute-done((f32[2,16,512]{2,1,0:T(8,128)S(1)}, f32[2,16,512]{2,1,0:T(8,128)S(1)}, u32[]{:S(2)}, u32[]{:S(2)}) %collective-permute-start.3) | collective-permute-done | bytes 65568 | tf_op jit(solution)/shard_map/ppermute | solution.py:149
  79.9 2.6 %shard_map.50 = bf16[2,8,2,16,896]{4,3,2,1,0:T(8,128)(2,1)} custom-call(bf16[256,896]{1,0:T(8,128)(2,1)S(1)} %shard_map.49.first_ref, bf16[8,2,16,2304]{3,2,1,0:T(8,128)(2,1)S(1)} %collective-permute-done.2.other_ref, bf16[1792,896]{1,0:T(8,128)(2,1)S(1)} %copy-done), custom_call_target="tpu_custom_call" | custom-call | bytes 4849664 | tf_op jit(solution)/shard_map/pallas_call | solution.py:23
  82.6 8.5 %all-to-all-start.2 = ((bf16[16,2,16,896]{3,2,1,0:T(8,128)(2,1)}), bf16[16,2,16,896]{3,2,1,0:T(8,128)(2,1)S(1)}, u32[]{:S(2)}, u32[]{:S(2)}) async-start(bf16[16,2,16,896]{3,2,1,0:T(8,128)(2,1)} %bitcast.1), calls=%async_computation.2 | async-start | bytes 1835008 | tf_op jit(solution)/shard_map/all_to_all | solution.py:33
  91.0 24.9 %all-gather = bf16[16,16,512]{2,1,0:T(8,128)(2,1)S(1)} all-gather(bf16[2,16,512]{2,1,0:T(8,128)(2,1)S(1)} %shard_map.52), channel_id=2, replica_groups=mesh['x'=4,'y_lo'=4,'y_hi'=2,'z'=8,'core'=2] {'z'}, dimensions={0}, use_global_device_ids=true | all-gather | bytes 294912 | tf_op jit(solution)/shard_map/all_gather | solution.py:178
  116.0 0.8 shard_map.53
  116.8 4.9 %all-to-all-start.3 = ((bf16[4,2,16,896]{3,2,1,0:T(8,128)(2,1)}), bf16[4,2,16,896]{3,2,1,0:T(8,128)(2,1)S(1)}, u32[]{:S(2)}, u32[]{:S(2)}) async-start(bf16[4,2,16,896]{3,2,1,0:T(8,128)(2,1)} %shard_map.53), calls=%async_computation.3 | async-start | bytes 458752 | tf_op jit(solution)/shard_map/all_to_all | solution.py:33
  121.7 1.9 %collective-permute-start.4 = (bf16[8,2,16,512]{3,2,1,0:T(8,128)(2,1)S(1)}, bf16[8,2,16,512]{3,2,1,0:T(8,128)(2,1)S(1)}, u32[]{:S(2)}, u32[]{:S(2)}) collective-permute-start(bf16[8,2,16,512]{3,2,1,0:T(8,128)(2,1)S(1)} %bitcast.3), channel_id=1, source_target_pairs={{0,1},{1,0},{2,3},{3,2},{4,5},{5,4},{6,7},{7,6},{8,9},{9,8},{10,11... | collective-permute-start | bytes 786440 | tf_op jit(solution)/shard_map/ppermute | solution.py:180
  123.7 4.0 %all-to-all-done.3 = bf16[4,2,16,896]{3,2,1,0:T(8,128)(2,1)S(1)} async-done(((bf16[4,2,16,896]{3,2,1,0:T(8,128)(2,1)}), bf16[4,2,16,896]{3,2,1,0:T(8,128)(2,1)S(1)}, u32[]{:S(2)}, u32[]{:S(2)}) %all-to-all-start.3) | async-done | bytes 229408 | tf_op jit(solution)/shard_map/all_to_all | solution.py:33
  127.7 14.9 %all_gather.11.grad_ref = bf16[16,2,16,896]{3,2,1,0:T(8,128)(2,1)S(1)} all-gather(bf16[4,2,16,896]{3,2,1,0:T(8,128)(2,1)S(1)} %all-to-all-done.3), channel_id=1, replica_groups=mesh['x'=4,'y_lo'=4,'y_hi'=2,'z'=8,'core'=2] {'x'}, dimensions={0}, use_global_device_ids=true | all-gather | bytes 1146880 | tf_op jit(solution)/shard_map/all_gather | solution.py:184
  142.6 1.7 %shard_map.54 = bf16[512,896]{1,0:T(8,128)(2,1)} custom-call(bf16[8,2,16,512]{3,2,1,0:T(8,128)(2,1)S(1)} %bitcast.4, bf16[8,2,16,512]{3,2,1,0:T(8,128)(2,1)S(1)} %collective-permute-done.4.other_ref, bf16[16,2,16,896]{3,2,1,0:T(8,128)(2,1)S(1)} %all_gather.11.grad_ref), custom_call_target="tpu_custom_call" | custom-call | bytes 1441792 | tf_op jit(solution)/shard_map/pallas_call | solution.py:23
  (11 shorter events, 0.1 us)
Async XLA Ops:
  0.0 21.8 %copy-start.1 = (bf16[256,512]{1,0:T(8,128)(2,1)S(1)}, bf16[256,512]{1,0:T(8,128)(2,1)}, u32[]{:S(2)}) copy-start(bf16[256,512]{1,0:T(8,128)(2,1)} %basis_ref.3) | copy-start | bytes 786436
  1.5 20.3 %all-to-all-start = ((bf16[16,2,16,256]{3,2,1,0:T(8,128)(2,1)}), bf16[16,2,16,256]{3,2,1,0:T(8,128)(2,1)S(1)}, u32[]{:S(2)}, u32[]{:S(2)}) async-start(bf16[16,2,16,256]{3,2,1,0:T(8,128)(2,1)} %broadcast_in_dim.8), calls=%async_computation | async-start | bytes 524288 | tf_op jit(solution)/shard_map/all_to_all | solution.py:33
  10.6 10.3 %collective-permute-start = (bf16[16,1792]{1,0:T(8,128)(2,1)}, bf16[16,1792]{1,0:T(8,128)(2,1)S(1)}, u32[]{:S(2)}, u32[]{:S(2)}) collective-permute-start(bf16[16,1792]{1,0:T(8,128)(2,1)} %own_ref.1), channel_id=1, source_target_pairs={{0,16},{16,0},{1,17},{17,1},{2,18},{18,2},{3,19},{19,3},{4,20},{20... | collective-permute-start | bytes 172040 | tf_op jit(solution)/shard_map/ppermute | solution.py:137
  21.0 0.8 copy-start.2
  22.1 3.8 %collective-permute-start.1 = (f32[256,512]{1,0:T(8,128)S(1)}, f32[256,512]{1,0:T(8,128)S(1)}, u32[]{:S(2)}, u32[]{:S(2)}) collective-permute-start(f32[256,512]{1,0:T(8,128)S(1)} %get-tuple-element.16), channel_id=1, source_target_pairs={{0,1},{1,0},{2,3},{3,2},{4,5},{5,4},{6,7},{7,6},{8,9},{9,8},{10,11... | collective-permute-start | bytes 1572872 | tf_op jit(solution)/shard_map/ppermute | solution.py:142
  26.0 48.4 %copy-start = (bf16[1792,896]{1,0:T(8,128)(2,1)S(1)}, bf16[1792,896]{1,0:T(8,128)(2,1)}, u32[]{:S(2)}) copy-start(bf16[1792,896]{1,0:T(8,128)(2,1)} %basis_ref.5) | copy-start | bytes 9633796
  67.5 12.4 %collective-permute-start.2 = (bf16[8,2,16,2304]{3,2,1,0:T(8,128)(2,1)S(1)}, bf16[8,2,16,2304]{3,2,1,0:T(8,128)(2,1)S(1)}, u32[]{:S(2)}, u32[]{:S(2)}) collective-permute-start(bf16[8,2,16,2304]{3,2,1,0:T(8,128)(2,1)S(1)} %all_to_all.20.own_ref.packed_ref), channel_id=1, source_target_pairs={{0,1},{1,0},{2,3},{3,2},{4,5},{5,4},{6,7},{7,6},{8,9},{9,8},{10,11... | collective-permute-start | bytes 3538952 | tf_op jit(solution)/shard_map/ppermute | solution.py:146
  69.5 10.4 %collective-permute-start.3 = (f32[2,16,512]{2,1,0:T(8,128)S(1)}, f32[2,16,512]{2,1,0:T(8,128)S(1)}, u32[]{:S(2)}, u32[]{:S(2)}) collective-permute-start(f32[2,16,512]{2,1,0:T(8,128)S(1)} %shard_map.51.own_ref), channel_id=1, source_target_pairs={{0,16},{16,0},{1,17},{17,1},{2,18},{18,2},{3,19},{19,3},{4,20},{20... | collective-permute-start | bytes 196616 | tf_op jit(solution)/shard_map/ppermute | solution.py:149
  82.6 33.4 %all-to-all-start.2 = ((bf16[16,2,16,896]{3,2,1,0:T(8,128)(2,1)}), bf16[16,2,16,896]{3,2,1,0:T(8,128)(2,1)S(1)}, u32[]{:S(2)}, u32[]{:S(2)}) async-start(bf16[16,2,16,896]{3,2,1,0:T(8,128)(2,1)} %bitcast.1), calls=%async_computation.2 | async-start | bytes 1835008 | tf_op jit(solution)/shard_map/all_to_all | solution.py:33
  116.8 10.9 %all-to-all-start.3 = ((bf16[4,2,16,896]{3,2,1,0:T(8,128)(2,1)}), bf16[4,2,16,896]{3,2,1,0:T(8,128)(2,1)S(1)}, u32[]{:S(2)}, u32[]{:S(2)}) async-start(bf16[4,2,16,896]{3,2,1,0:T(8,128)(2,1)} %shard_map.53), calls=%async_computation.3 | async-start | bytes 458752 | tf_op jit(solution)/shard_map/all_to_all | solution.py:33
  121.7 20.8 %collective-permute-start.4 = (bf16[8,2,16,512]{3,2,1,0:T(8,128)(2,1)S(1)}, bf16[8,2,16,512]{3,2,1,0:T(8,128)(2,1)S(1)}, u32[]{:S(2)}, u32[]{:S(2)}) collective-permute-start(bf16[8,2,16,512]{3,2,1,0:T(8,128)(2,1)S(1)} %bitcast.3), channel_id=1, source_target_pairs={{0,1},{1,0},{2,3},{3,2},{4,5},{5,4},{6,7},{7,6},{8,9},{9,8},{10,11... | collective-permute-start | bytes 786440 | tf_op jit(solution)/shard_map/ppermute | solution.py:180

commit v3 on v2

--- a/solution.py
+++ b/solution.py
@@ -42,13 +42,12 @@
 
 
 def pack(grads_ref, keep_ref, recv_ref, out_ref):
-    count = out_ref.shape[0]
-    half, rows, depth = grads_ref.shape
+    count, rows, _ = out_ref.shape
+    depth = grads_ref.shape[1]
     for i in range(count):
-        for j in range(half):
-            part = slice((j * count + i) * rows, (j * count + i + 1) * rows)
-            out_ref[i, j, :, :depth] = grads_ref[j]
-            out_ref[i, j, :, depth:] = (keep_ref[part] + recv_ref[part]).astype(BF16)
+        part = slice(i * rows, (i + 1) * rows)
+        out_ref[i, :, :depth] = grads_ref[...]
+        out_ref[i, :, depth:] = (keep_ref[part] + recv_ref[part]).astype(BF16)
 
 
 def total_of(parts):
@@ -59,17 +58,7 @@
 
 
 def add_acts(packed_ref, out_ref):
-    out_ref[...] = total_of(packed_ref[:, :, :, packed_ref.shape[3] - out_ref.shape[2]:])
-
-
-def add_far(own_ref, far_ref, out_ref):
-    out_ref[...] = (own_ref[...] + far_ref[...]).astype(BF16)
-
-
-def place(own_ref, other_ref, out_ref):
-    here = lax.axis_index("y_hi")
-    out_ref[pl.ds(here, 1)] = own_ref[...][None]
-    out_ref[pl.ds(1 - here, 1)] = other_ref[...][None]
+    out_ref[...] = total_of(packed_ref[:, :, packed_ref.shape[2] - out_ref.shape[1]:]).astype(BF16)
 
 
 def add_grads(parts_ref, out_ref):
@@ -94,31 +83,30 @@
 
 def other_product(first_ref, other_ref, basis_ref, out_ref, sums_ref):
     step = pl.program_id(0)
-    halves, count, _, rows, width = out_ref.shape
+    core = lax.axis_index("core")
+    count, _, rows, width = out_ref.shape
     block = other_ref[...].reshape(sums_ref.shape[0], STEP)
     part = jnp.dot(block, basis_ref[...], preferred_element_type=F32)
 
     @pl.when(step == 0)
     def _():
         sums_ref[...] = part
-        first = first_ref[...].reshape(count, halves, rows, width)
-        for j in range(halves):
-            out_ref[j, :, 0] = first[:, j]
+        out_ref[:, pl.ds(core, 1)] = first_ref[...].reshape(count, 1, rows, width)
 
     @pl.when(step == pl.num_programs(0) - 1)
     def _():
-        last = (sums_ref[...] + part).astype(BF16).reshape(count, halves, rows, width)
-        for j in range(halves):
-            out_ref[j, :, 1] = last[:, j]
+        last = (sums_ref[...] + part).astype(BF16)
+        out_ref[:, pl.ds(1 - core, 1)] = last.reshape(count, 1, rows, width)
 
 
-def correct(own_ref, other_ref, grad_ref, out_ref):
+def correct(near_ref, far_ref, grad_ref, out_ref):
     count = grad_ref.shape[0] // SEQS
+    seq = lax.axis_index("y_hi")
     total = None
-    for seq in range(SEQS):
-        acts = jnp.stack([own_ref[:, seq], other_ref[:, seq]], axis=1)
+    for which, ref in ((seq, near_ref), (1 - seq, far_ref)):
+        acts = jnp.stack([ref[0], ref[1]], axis=1)
         acts = acts.reshape(-1, acts.shape[-1])
-        grads = grad_ref[seq * count:(seq + 1) * count]
+        grads = grad_ref[pl.ds(which * count, count)]
         grads = grads.reshape(-1, grads.shape[-1])
         product = lax.dot_general(acts, grads, (((0,), (0,)), ((), ())), preferred_element_type=F32)
         square = product * product
@@ -134,22 +122,17 @@
 
     acts = activations.reshape(1, 2, rows, acts_in)
     acts = spread(jnp.broadcast_to(acts, (16, 2, rows, acts_in)), NARROW)
-    grads_far = lax.ppermute(out_grads, "y_hi", PAIR)
-    grads = call(place, shape((2, rows, depth), BF16), out_grads, grads_far)
-    acts, grads = lax.optimization_barrier((acts, grads))
     half = shape((16 * rows, acts_out), F32)
     keep, send = call(act_product, (half, half), acts, act_basis)
     recv = lax.ppermute(send, "core", PAIR)
 
-    packed = call(pack, shape((8, 2, rows, depth + acts_out), BF16), grads, keep, recv)
-    packed = spread(packed, "z")
+    packed = call(pack, shape((16, rows, depth + acts_out), BF16), out_grads, keep, recv)
+    packed = spread(packed, PLANE)
     packed_other = lax.ppermute(packed, "core", PAIR)
-
-    act_near = call(add_acts, shape((2, rows, acts_out), F32), packed)
-    act_far = lax.ppermute(act_near, "y_hi", PAIR)
+    act_rot = call(add_acts, shape((rows, acts_out), BF16), packed)
 
     specs = [
-        pl.BlockSpec((8, 2, rows, STEP), lambda k: (0, 0, 0, k)),
+        pl.BlockSpec((16, rows, STEP), lambda k: (0, 0, k)),
         pl.BlockSpec((STEP, width), lambda k: (k, 0)),
     ]
     more = dict(grid=(depth // STEP,), scratch_shapes=[pltpu.VMEM((16 * rows, width), F32)])
@@ -164,25 +147,26 @@
     )
     grad_part = call(
         other_product,
-        shape((2, 8, 2, rows, width), BF16),
+        shape((16, 2, rows, width), BF16),
         first,
         packed_other,
         grad_basis,
         in_specs=[pl.BlockSpec((16 * rows, width), lambda k: (0, 0))] + specs,
-        out_specs=pl.BlockSpec((2, 8, 2, rows, width), lambda k: (0, 0, 0, 0, 0)),
+        out_specs=pl.BlockSpec((16, 2, rows, width), lambda k: (0, 0, 0, 0)),
         **more,
     )
-    act_two = call(add_far, shape((2, rows, acts_out), BF16), act_near, act_far)
-    grad_part, act_two = lax.optimization_barrier((grad_part, act_two))
-    grad_parts = spread(grad_part.reshape(16, 2, rows, width), NARROW)
-    act_own = lax.all_gather(act_two, "z", axis=0)
-    grad_parts, act_own = lax.optimization_barrier((grad_parts, act_own))
-    act_other = lax.ppermute(act_own, "core", PAIR)
+    grad_part, act_rot = lax.optimization_barrier((grad_part, act_rot))
+    grad_parts = spread(grad_part, NARROW)
+    act_near = lax.all_gather(act_rot, "z", axis=0)
+    grad_parts, act_near = lax.optimization_barrier((grad_parts, act_near))
 
     grad_rot = call(add_grads, shape((4, 2, rows, width), BF16), grad_parts)
     grad_rot = spread(grad_rot, "y_lo")
+    act_near = lax.all_gather(act_near, "core", axis=0)
+    act_far = lax.ppermute(act_near, "y_hi", PAIR)
+    grad_rot, act_near = lax.optimization_barrier((grad_rot, act_near))
     grad_rot = lax.all_gather(grad_rot, "x", axis=0, tiled=True)
-    return call(correct, shape((acts_out, width), BF16), act_own, act_other, grad_rot)
+    return call(correct, shape((acts_out, width), BF16), act_near, act_far, grad_rot)
 
 
 def solution(mesh):

time: 145 us -> 139 us (0.959)
  blocking collectives: 81.3 us -> 107 us
  starting transfers between devices: 36.9 us -> 16.4 us
  waiting for transfers between devices: 16.3 us -> 5.38 us
    all_to_all x1 -> x2, blocking collectives: 41.5 us -> 66.4 us  [spread(): return lax.all_to_all(copies, axes, 0, 0)]
    all_to_all x3 -> x2, starting transfers between devices: 22.6 us -> 9.64 us  [spread(): return lax.all_to_all(copies, axes, 0, 0)]
    ppermute x2 -> x0, waiting for transfers between devices: 6.63 us -> none  [the longest x1 6.63 us: shards(): grads_far = lax.ppermute(out_grads, 'y_hi', PAIR)]
    ppermute x2 -> x0, starting transfers between devices: 5.59 us -> none  [the longest x1 3.68 us: shards(): grads_far = lax.ppermute(out_grads, 'y_hi', PAIR)]
    all_to_all x3 -> x2, waiting for transfers between devices: 4.04 us -> 1.06 us  [spread(): return lax.all_to_all(copies, axes, 0, 0)]
    ppermute x1, waiting for transfers between devices: 3.74 us -> 1.39 us  [shards(): act_far = lax.ppermute(act_near, 'y_hi', PAIR)]
    ppermute x1, starting transfers between devices: 4.94 us -> 2.91 us  [shards(): act_far = lax.ppermute(act_near, 'y_hi', PAIR)]
    all_gather x1 -> x2, blocking collectives: 24.9 us -> 26.6 us  [the longest x1 24.6 us: shards(): act_near = lax.all_gather(act_rot, 'z', axis=0)]
  transfers between devices with their start and end apart: 8 -> 5, of which waited for: 4 -> 4; matrix products, arithmetic and copies ran while one was open for 0% -> 0% of each run, Pallas kernels for 1% -> 1%
where the time goes in v3:
time: 139 us; the launch traced here: 138 us
  blocking collectives  107 us (77%)
  starting transfers between devices  16.4 us (12%)
  Pallas kernels  7.25 us (5%)
  waiting for transfers between devices  5.38 us (4%)
  local copies, waits for them, and re-layouts  1.7 us (1%)
    all_to_all x2, blocking collectives, spread(): return lax.all_to_all(copies, axes, 0, 0)  66.4 us
    all_gather x1, blocking collectives, shards(): act_near = lax.all_gather(act_rot, 'z', axis=0)  24.6 us
    all_gather x1, blocking collectives, shards(): grad_rot = lax.all_gather(grad_rot, 'x', axis=0, tiled=True)  14.3 us
    all_to_all x2, starting transfers between devices, spread(): return lax.all_to_all(copies, axes, 0, 0)  9.64 us
    pallas_call x7, Pallas kernels, call(): pl.pallas_call(body, out_shape=outs, compiler_params=pltpu.CompilerParams...  7.25 us
    ppermute x1, starting transfers between devices, shards(): act_far = lax.ppermute(act_near, 'y_hi', PAIR)  2.91 us
  transfers between devices with their start and end apart: 5, of which 4 were waited for; matrix products, arithmetic and copies ran while one was open for 0% of the time, Pallas kernels for 1%

profile of v3, /device:TPU:8, one launch (start us, length us, event | category | flops | bytes accessed | tf_op | source)
XLA Modules:
  0.0 138.1 jit_solution(12526637921942655064)
XLA Ops:
  0.0 0.7 broadcast_in_dim.8
  0.8 16.8 %all_to_all.20.acts_ref = bf16[16,2,16,256]{3,2,1,0:T(8,128)(2,1)S(1)} all-to-all(bf16[16,2,16,256]{3,2,1,0:T(8,128)(2,1)S(1)} %broadcast_in_dim.8), channel_id=1, replica_groups=mesh['x'=4,'y_lo'=4,'y_hi'=2,'z'=8,'core'=2] {'x','y_lo'}, dimensions={0} | all-to-all | bytes 524288 | tf_op jit(solution)/shard_map/all_to_all | solution.py:33
  17.5 0.9 copy-done.1
  18.5 0.3 shard_map.46
  18.8 1.9 %collective-permute-start = (f32[256,512]{1,0:T(8,128)S(1)}, f32[256,512]{1,0:T(8,128)S(1)}, u32[]{:S(2)}, u32[]{:S(2)}) collective-permute-start(f32[256,512]{1,0:T(8,128)S(1)} %get-tuple-element.14), channel_id=1, source_target_pairs={{0,1},{1,0},{2,3},{3,2},{4,5},{5,4},{6,7},{7,6},{8,9},{9,8},{10,11... | collective-permute-start | bytes 1572872 | tf_op jit(solution)/shard_map/ppermute | solution.py:127
  20.7 1.9 %collective-permute-done.recv_ref = f32[256,512]{1,0:T(8,128)S(1)} collective-permute-done((f32[256,512]{1,0:T(8,128)S(1)}, f32[256,512]{1,0:T(8,128)S(1)}, u32[]{:S(2)}, u32[]{:S(2)}) %collective-permute-start) | collective-permute-done | bytes 524320 | tf_op jit(solution)/shard_map/ppermute | solution.py:127
  22.6 0.1 shard_map.47
  22.7 0.0 copy-start
  22.7 49.6 %all_to_all.21.own_ref.packed_ref = bf16[16,16,2304]{2,1,0:T(8,128)(2,1)S(1)} all-to-all(bf16[16,16,2304]{2,1,0:T(8,128)(2,1)S(1)} %shard_map.47), channel_id=1, replica_groups=mesh['x'=4,'y_lo'=4,'y_hi'=2,'z'=8,'core'=2] {'y_hi','z'}, dimensions={0} | all-to-all | bytes 2359296 | tf_op jit(solution)/shard_map/all_to_all | solution.py:33
  72.3 1.9 %collective-permute-start.1 = (bf16[16,16,2304]{2,1,0:T(8,128)(2,1)S(1)}, bf16[16,16,2304]{2,1,0:T(8,128)(2,1)S(1)}, u32[]{:S(2)}, u32[]{:S(2)}) collective-permute-start(bf16[16,16,2304]{2,1,0:T(8,128)(2,1)S(1)} %all_to_all.21.own_ref.packed_ref), channel_id=1, source_target_pairs={{0,1},{1,0},{2,3},{3,2},{4,5},{5,4},{6,7},{7,6},{8,9},{9,8},{10,11... | collective-permute-start | bytes 3538952 | tf_op jit(solution)/shard_map/ppermute | solution.py:131
  74.3 1.7 %shard_map.48.first_ref = bf16[256,896]{1,0:T(8,128)(2,1)S(1)} custom-call(bf16[16,16,2304]{2,1,0:T(8,128)(2,1)S(1)} %all_to_all.21.own_ref.packed_ref, bf16[1792,896]{1,0:T(8,128)(2,1)S(1)} %copy-done), custom_call_target="tpu_custom_call" | custom-call | bytes 4390912 | tf_op jit(solution)/shard_map/pallas_call | solution.py:23
  76.0 1.0 collective-permute-done.1.other_ref
  77.0 2.6 %shard_map.49 = bf16[16,2,16,896]{3,2,1,0:T(8,128)(2,1)} custom-call(bf16[256,896]{1,0:T(8,128)(2,1)S(1)} %shard_map.48.first_ref, bf16[16,16,2304]{2,1,0:T(8,128)(2,1)S(1)} %collective-permute-done.1.other_ref, bf16[1792,896]{1,0:T(8,128)(2,1)S(1)} %copy-done), custom_call_target="tpu_custom_call" | custom-call | bytes 4849664 | tf_op jit(solution)/shard_map/pallas_call | solution.py:23
  79.6 4.6 %all-to-all-start.2 = ((bf16[16,2,16,896]{3,2,1,0:T(8,128)(2,1)}), bf16[16,2,16,896]{3,2,1,0:T(8,128)(2,1)S(1)}, u32[]{:S(2)}, u32[]{:S(2)}) async-start(bf16[16,2,16,896]{3,2,1,0:T(8,128)(2,1)} %shard_map.49), calls=%async_computation.2 | async-start | bytes 1835008 | tf_op jit(solution)/shard_map/all_to_all | solution.py:33
  84.2 24.6 %all-gather = bf16[128,512]{1,0:T(8,128)(2,1)S(1)} all-gather(bf16[16,512]{1,0:T(8,128)(2,1)S(1)} %shard_map.50), channel_id=2, replica_groups=mesh['x'=4,'y_lo'=4,'y_hi'=2,'z'=8,'core'=2] {'z'}, dimensions={0}, use_global_device_ids=true | all-gather | bytes 147456 | tf_op jit(solution)/shard_map/all_gather | solution.py:160
  108.8 0.0 all-to-all-done.2.parts_ref
  108.8 0.8 shard_map.51
  109.6 5.1 %all-to-all-start.3 = ((bf16[4,2,16,896]{3,2,1,0:T(8,128)(2,1)}), bf16[4,2,16,896]{3,2,1,0:T(8,128)(2,1)S(1)}, u32[]{:S(2)}, u32[]{:S(2)}) async-start(bf16[4,2,16,896]{3,2,1,0:T(8,128)(2,1)} %shard_map.51), calls=%async_computation.3 | async-start | bytes 458752 | tf_op jit(solution)/shard_map/all_to_all | solution.py:33
  114.7 2.0 %all-gather.1 = bf16[16,16,512]{2,1,0:T(8,128)(2,1)S(1)} all-gather(bf16[8,16,512]{2,1,0:T(8,128)(2,1)S(1)} %bitcast.5), channel_id=3, replica_groups=mesh['x'=4,'y_lo'=4,'y_hi'=2,'z'=8,'core'=2] {'core'}, dimensions={0}, use_global_device_ids=true | all-gather | bytes 393216 | tf_op jit(solution)/shard_map/all_gather | solution.py:165
  116.7 2.9 %collective-permute-start.2 = (bf16[2,8,16,512]{3,2,1,0:T(8,128)(2,1)S(1)}, bf16[2,8,16,512]{3,2,1,0:T(8,128)(2,1)S(1)}, u32[]{:S(2)}, u32[]{:S(2)}) collective-permute-start(bf16[2,8,16,512]{3,2,1,0:T(8,128)(2,1)S(1)} %bitcast.3), channel_id=1, source_target_pairs={{0,16},{16,0},{1,17},{17,1},{2,18},{18,2},{3,19},{19,3},{4,20},{20... | collective-permute-start | bytes 786440 | tf_op jit(solution)/shard_map/ppermute | solution.py:166
  119.6 1.1 all-to-all-done.3
  120.6 14.3 %all_gather.19.grad_ref = bf16[16,2,16,896]{3,2,1,0:T(8,128)(2,1)S(1)} all-gather(bf16[4,2,16,896]{3,2,1,0:T(8,128)(2,1)S(1)} %all-to-all-done.3), channel_id=1, replica_groups=mesh['x'=4,'y_lo'=4,'y_hi'=2,'z'=8,'core'=2] {'x'}, dimensions={0}, use_global_device_ids=true | all-gather | bytes 1146880 | tf_op jit(solution)/shard_map/all_gather | solution.py:168
  135.0 1.4 %collective-permute-done.2.far_ref = bf16[2,8,16,512]{3,2,1,0:T(8,128)(2,1)S(1)} collective-permute-done((bf16[2,8,16,512]{3,2,1,0:T(8,128)(2,1)S(1)}, bf16[2,8,16,512]{3,2,1,0:T(8,128)(2,1)S(1)}, u32[]{:S(2)}, u32[]{:S(2)}) %collective-permute-start.2) | collective-permute-done | bytes 262176 | tf_op jit(solution)/shard_map/ppermute | solution.py:166
  136.4 1.7 %shard_map.52 = bf16[512,896]{1,0:T(8,128)(2,1)} custom-call(bf16[2,8,16,512]{3,2,1,0:T(8,128)(2,1)S(1)} %bitcast.4, bf16[2,8,16,512]{3,2,1,0:T(8,128)(2,1)S(1)} %collective-permute-done.2.far_ref, bf16[16,2,16,896]{3,2,1,0:T(8,128)(2,1)S(1)} %all_gather.19.grad_ref), custom_call_target="tpu_custom_call" | custom-call | bytes 1441792 | tf_op jit(solution)/shard_map/pallas_call | solution.py:23
  (5 shorter events, 0.1 us)
Async XLA Ops:
  0.0 22.6 %copy-start.2 = (bf16[16,1792]{1,0:T(8,128)(2,1)S(1)}, bf16[16,1792]{1,0:T(8,128)(2,1)}, u32[]{:S(2)}) copy-start(bf16[16,1792]{1,0:T(8,128)(2,1)} %grads_ref.1) | copy-start | bytes 172036
  17.5 1.0 copy-start.1
  18.8 3.8 %collective-permute-start = (f32[256,512]{1,0:T(8,128)S(1)}, f32[256,512]{1,0:T(8,128)S(1)}, u32[]{:S(2)}, u32[]{:S(2)}) collective-permute-start(f32[256,512]{1,0:T(8,128)S(1)} %get-tuple-element.14), channel_id=1, source_target_pairs={{0,1},{1,0},{2,3},{3,2},{4,5},{5,4},{6,7},{7,6},{8,9},{9,8},{10,11... | collective-permute-start | bytes 1572872 | tf_op jit(solution)/shard_map/ppermute | solution.py:127
  22.7 51.6 %copy-start = (bf16[1792,896]{1,0:T(8,128)(2,1)S(1)}, bf16[1792,896]{1,0:T(8,128)(2,1)}, u32[]{:S(2)}) copy-start(bf16[1792,896]{1,0:T(8,128)(2,1)} %basis_ref.5) | copy-start | bytes 9633796
  72.3 4.7 %collective-permute-start.1 = (bf16[16,16,2304]{2,1,0:T(8,128)(2,1)S(1)}, bf16[16,16,2304]{2,1,0:T(8,128)(2,1)S(1)}, u32[]{:S(2)}, u32[]{:S(2)}) collective-permute-start(bf16[16,16,2304]{2,1,0:T(8,128)(2,1)S(1)} %all_to_all.21.own_ref.packed_ref), channel_id=1, source_target_pairs={{0,1},{1,0},{2,3},{3,2},{4,5},{5,4},{6,7},{7,6},{8,9},{9,8},{10,11... | collective-permute-start | bytes 3538952 | tf_op jit(solution)/shard_map/ppermute | solution.py:131
  79.6 29.1 %all-to-all-start.2 = ((bf16[16,2,16,896]{3,2,1,0:T(8,128)(2,1)}), bf16[16,2,16,896]{3,2,1,0:T(8,128)(2,1)S(1)}, u32[]{:S(2)}, u32[]{:S(2)}) async-start(bf16[16,2,16,896]{3,2,1,0:T(8,128)(2,1)} %shard_map.49), calls=%async_computation.2 | async-start | bytes 1835008 | tf_op jit(solution)/shard_map/all_to_all | solution.py:33
  109.6 11.0 %all-to-all-start.3 = ((bf16[4,2,16,896]{3,2,1,0:T(8,128)(2,1)}), bf16[4,2,16,896]{3,2,1,0:T(8,128)(2,1)S(1)}, u32[]{:S(2)}, u32[]{:S(2)}) async-start(bf16[4,2,16,896]{3,2,1,0:T(8,128)(2,1)} %shard_map.51), calls=%async_computation.3 | async-start | bytes 458752 | tf_op jit(solution)/shard_map/all_to_all | solution.py:33
  116.7 19.7 %collective-permute-start.2 = (bf16[2,8,16,512]{3,2,1,0:T(8,128)(2,1)S(1)}, bf16[2,8,16,512]{3,2,1,0:T(8,128)(2,1)S(1)}, u32[]{:S(2)}, u32[]{:S(2)}) collective-permute-start(bf16[2,8,16,512]{3,2,1,0:T(8,128)(2,1)S(1)} %bitcast.3), channel_id=1, source_target_pairs={{0,16},{16,0},{1,17},{17,1},{2,18},{18,2},{3,19},{19,3},{4,20},{20... | collective-permute-start | bytes 786440 | tf_op jit(solution)/shard_map/ppermute | solution.py:166

commit v4 on v3

--- a/solution.py
+++ b/solution.py
@@ -1,3 +1,5 @@
+import functools
+
 import jax
 import jax.numpy as jnp
 from jax import lax
@@ -33,12 +35,11 @@
     return lax.all_to_all(copies, axes, 0, 0)
 
 
-def act_product(acts_ref, basis_ref, keep_ref, send_ref):
+def act_product(flip, acts_ref, basis_ref, out_ref):
     core = lax.axis_index("core")
-    for ref, part in ((keep_ref, core), (send_ref, 1 - core)):
-        rows = acts_ref[:, pl.ds(part, 1)]
-        rows = rows.reshape(ref.shape[0], basis_ref.shape[0])
-        ref[...] = jnp.dot(rows, basis_ref[...], preferred_element_type=F32)
+    rows = acts_ref[:, pl.ds(1 - core if flip else core, 1)]
+    rows = rows.reshape(out_ref.shape[0], basis_ref.shape[0])
+    out_ref[...] = jnp.dot(rows, basis_ref[...], preferred_element_type=F32)
 
 
 def pack(grads_ref, keep_ref, recv_ref, out_ref):
@@ -123,8 +124,9 @@
     acts = activations.reshape(1, 2, rows, acts_in)
     acts = spread(jnp.broadcast_to(acts, (16, 2, rows, acts_in)), NARROW)
     half = shape((16 * rows, acts_out), F32)
-    keep, send = call(act_product, (half, half), acts, act_basis)
+    send = call(functools.partial(act_product, True), half, acts, act_basis)
     recv = lax.ppermute(send, "core", PAIR)
+    keep = call(functools.partial(act_product, False), half, acts, act_basis)
 
     packed = call(pack, shape((16, rows, depth + acts_out), BF16), out_grads, keep, recv)
     packed = spread(packed, PLANE)
@@ -166,7 +168,17 @@
     act_far = lax.ppermute(act_near, "y_hi", PAIR)
     grad_rot, act_near = lax.optimization_barrier((grad_rot, act_near))
     grad_rot = lax.all_gather(grad_rot, "x", axis=0, tiled=True)
-    return call(correct, shape((acts_out, width), BF16), act_near, act_far, grad_rot)
+    act_spec = pl.BlockSpec((2, 8, rows, acts_out // 2), lambda k: (0, 0, 0, k))
+    return call(
+        correct,
+        shape((acts_out, width), BF16),
+        act_near,
+        act_far,
+        grad_rot,
+        grid=(2,),
+        in_specs=[act_spec, act_spec, pl.BlockSpec((16, 2, rows, width), lambda k: (0, 0, 0, 0))],
+        out_specs=pl.BlockSpec((acts_out // 2, width), lambda k: (k, 0)),
+    )
 
 
 def solution(mesh):

time: 139 us -> 139 us (level)
    pallas_call x7 -> x8, Pallas kernels: 7.25 us -> 7.46 us  [call(): pl.pallas_call(body, out_shape=outs, compiler_params=pltpu.CompilerParams...]
where the time goes in v4:
time: 139 us; the launch traced here: 138 us
  blocking collectives  107 us (77%)
  starting transfers between devices  16.4 us (12%)
  Pallas kernels  7.46 us (5%)
  waiting for transfers between devices  5.11 us (4%)
  local copies, waits for them, and re-layouts  1.7 us (1%)
    all_to_all x2, blocking collectives, spread(): return lax.all_to_all(copies, axes, 0, 0)  66.5 us
    all_gather x1, blocking collectives, shards(): act_near = lax.all_gather(act_rot, 'z', axis=0)  24.6 us
    all_gather x1, blocking collectives, shards(): grad_rot = lax.all_gather(grad_rot, 'x', axis=0, tiled=True)  14.4 us
    all_to_all x2, starting transfers between devices, spread(): return lax.all_to_all(copies, axes, 0, 0)  9.65 us
    pallas_call x8, Pallas kernels, call(): pl.pallas_call(body, out_shape=outs, compiler_params=pltpu.CompilerParams...  7.46 us
    ppermute x1, starting transfers between devices, shards(): act_far = lax.ppermute(act_near, 'y_hi', PAIR)  2.91 us
  transfers between devices with their start and end apart: 5, of which 4 were waited for; matrix products, arithmetic and copies ran while one was open for 0% of the time, Pallas kernels for 1%

profile of v4, /device:TPU:8, one launch (start us, length us, event | category | flops | bytes accessed | tf_op | source)
XLA Modules:
  0.0 138.2 jit_solution(12629129386004440019)
XLA Ops:
  0.0 0.7 broadcast_in_dim.8
  0.7 0.0 copy-start.2
  0.8 16.9 %all_to_all.20.acts_ref = bf16[16,2,16,256]{3,2,1,0:T(8,128)(2,1)S(1)} all-to-all(bf16[16,2,16,256]{3,2,1,0:T(8,128)(2,1)S(1)} %broadcast_in_dim.8), channel_id=1, replica_groups=mesh['x'=4,'y_lo'=4,'y_hi'=2,'z'=8,'core'=2] {'x','y_lo'}, dimensions={0} | all-to-all | bytes 524288 | tf_op jit(solution)/shard_map/all_to_all | solution.py:35
  17.7 0.9 copy-done.1
  18.6 0.2 shard_map.47
  18.9 1.9 %collective-permute-start = (f32[256,512]{1,0:T(8,128)S(1)}, f32[256,512]{1,0:T(8,128)S(1)}, u32[]{:S(2)}, u32[]{:S(2)}) collective-permute-start(f32[256,512]{1,0:T(8,128)S(1)} %shard_map.47), channel_id=1, source_target_pairs={{0,1},{1,0},{2,3},{3,2},{4,5},{5,4},{6,7},{7,6},{8,9},{9,8},{10,11... | collective-permute-start | bytes 1572872 | tf_op jit(solution)/shard_map/ppermute | solution.py:128
  20.8 0.2 shard_map.46.keep_ref
  21.0 1.7 %collective-permute-done.recv_ref = f32[256,512]{1,0:T(8,128)S(1)} collective-permute-done((f32[256,512]{1,0:T(8,128)S(1)}, f32[256,512]{1,0:T(8,128)S(1)}, u32[]{:S(2)}, u32[]{:S(2)}) %collective-permute-start) | collective-permute-done | bytes 524320 | tf_op jit(solution)/shard_map/ppermute | solution.py:128
  22.7 0.1 shard_map.48
  22.8 49.6 %all_to_all.21.own_ref.packed_ref = bf16[16,16,2304]{2,1,0:T(8,128)(2,1)S(1)} all-to-all(bf16[16,16,2304]{2,1,0:T(8,128)(2,1)S(1)} %shard_map.48), channel_id=1, replica_groups=mesh['x'=4,'y_lo'=4,'y_hi'=2,'z'=8,'core'=2] {'y_hi','z'}, dimensions={0} | all-to-all | bytes 2359296 | tf_op jit(solution)/shard_map/all_to_all | solution.py:35
  72.4 1.9 %collective-permute-start.1 = (bf16[16,16,2304]{2,1,0:T(8,128)(2,1)S(1)}, bf16[16,16,2304]{2,1,0:T(8,128)(2,1)S(1)}, u32[]{:S(2)}, u32[]{:S(2)}) collective-permute-start(bf16[16,16,2304]{2,1,0:T(8,128)(2,1)S(1)} %all_to_all.21.own_ref.packed_ref), channel_id=1, source_target_pairs={{0,1},{1,0},{2,3},{3,2},{4,5},{5,4},{6,7},{7,6},{8,9},{9,8},{10,11... | collective-permute-start | bytes 3538952 | tf_op jit(solution)/shard_map/ppermute | solution.py:133
  74.3 1.7 %shard_map.49.first_ref = bf16[256,896]{1,0:T(8,128)(2,1)S(1)} custom-call(bf16[16,16,2304]{2,1,0:T(8,128)(2,1)S(1)} %all_to_all.21.own_ref.packed_ref, bf16[1792,896]{1,0:T(8,128)(2,1)S(1)} %copy-done), custom_call_target="tpu_custom_call" | custom-call | bytes 4390912 | tf_op jit(solution)/shard_map/pallas_call | solution.py:25
  76.0 1.0 collective-permute-done.1.other_ref
  77.1 2.6 %shard_map.50 = bf16[16,2,16,896]{3,2,1,0:T(8,128)(2,1)} custom-call(bf16[256,896]{1,0:T(8,128)(2,1)S(1)} %shard_map.49.first_ref, bf16[16,16,2304]{2,1,0:T(8,128)(2,1)S(1)} %collective-permute-done.1.other_ref, bf16[1792,896]{1,0:T(8,128)(2,1)S(1)} %copy-done), custom_call_target="tpu_custom_call" | custom-call | bytes 4849664 | tf_op jit(solution)/shard_map/pallas_call | solution.py:25
  79.7 4.6 %all-to-all-start.2 = ((bf16[16,2,16,896]{3,2,1,0:T(8,128)(2,1)}), bf16[16,2,16,896]{3,2,1,0:T(8,128)(2,1)S(1)}, u32[]{:S(2)}, u32[]{:S(2)}) async-start(bf16[16,2,16,896]{3,2,1,0:T(8,128)(2,1)} %shard_map.50), calls=%async_computation.2 | async-start | bytes 1835008 | tf_op jit(solution)/shard_map/all_to_all | solution.py:35
  84.3 24.6 %all-gather = bf16[128,512]{1,0:T(8,128)(2,1)S(1)} all-gather(bf16[16,512]{1,0:T(8,128)(2,1)S(1)} %shard_map.51), channel_id=2, replica_groups=mesh['x'=4,'y_lo'=4,'y_hi'=2,'z'=8,'core'=2] {'z'}, dimensions={0}, use_global_device_ids=true | all-gather | bytes 147456 | tf_op jit(solution)/shard_map/all_gather | solution.py:162
  108.8 0.8 shard_map.52
  109.6 5.1 %all-to-all-start.3 = ((bf16[4,2,16,896]{3,2,1,0:T(8,128)(2,1)}), bf16[4,2,16,896]{3,2,1,0:T(8,128)(2,1)S(1)}, u32[]{:S(2)}, u32[]{:S(2)}) async-start(bf16[4,2,16,896]{3,2,1,0:T(8,128)(2,1)} %shard_map.52), calls=%async_computation.3 | async-start | bytes 458752 | tf_op jit(solution)/shard_map/all_to_all | solution.py:35
  114.7 2.0 %all-gather.1 = bf16[16,16,512]{2,1,0:T(8,128)(2,1)S(1)} all-gather(bf16[8,16,512]{2,1,0:T(8,128)(2,1)S(1)} %bitcast.5), channel_id=3, replica_groups=mesh['x'=4,'y_lo'=4,'y_hi'=2,'z'=8,'core'=2] {'core'}, dimensions={0}, use_global_device_ids=true | all-gather | bytes 393216 | tf_op jit(solution)/shard_map/all_gather | solution.py:167
  116.7 2.9 %collective-permute-start.2 = (bf16[2,8,16,512]{3,2,1,0:T(8,128)(2,1)S(1)}, bf16[2,8,16,512]{3,2,1,0:T(8,128)(2,1)S(1)}, u32[]{:S(2)}, u32[]{:S(2)}) collective-permute-start(bf16[2,8,16,512]{3,2,1,0:T(8,128)(2,1)S(1)} %bitcast.3), channel_id=1, source_target_pairs={{0,16},{16,0},{1,17},{17,1},{2,18},{18,2},{3,19},{19,3},{4,20},{20... | collective-permute-start | bytes 786440 | tf_op jit(solution)/shard_map/ppermute | solution.py:168
  119.6 1.1 all-to-all-done.3
  120.7 14.4 %all_gather.19.grad_ref = bf16[16,2,16,896]{3,2,1,0:T(8,128)(2,1)S(1)} all-gather(bf16[4,2,16,896]{3,2,1,0:T(8,128)(2,1)S(1)} %all-to-all-done.3), channel_id=1, replica_groups=mesh['x'=4,'y_lo'=4,'y_hi'=2,'z'=8,'core'=2] {'x'}, dimensions={0}, use_global_device_ids=true | all-gather | bytes 1146880 | tf_op jit(solution)/shard_map/all_gather | solution.py:170
  135.0 1.4 collective-permute-done.2.far_ref
  136.4 1.8 %shard_map.53 = bf16[512,896]{1,0:T(8,128)(2,1)} custom-call(bf16[2,8,16,512]{3,2,1,0:T(8,128)(2,1)S(1)} %bitcast.4, bf16[2,8,16,512]{3,2,1,0:T(8,128)(2,1)S(1)} %collective-permute-done.2.far_ref, bf16[16,2,16,896]{3,2,1,0:T(8,128)(2,1)S(1)} %all_gather.19.grad_ref), custom_call_target="tpu_custom_call" | custom-call | bytes 1441792 | tf_op jit(solution)/shard_map/pallas_call | solution.py:25
  (6 shorter events, 0.1 us)
Async XLA Ops:
  0.7 21.9 %copy-start.2 = (bf16[16,1792]{1,0:T(8,128)(2,1)S(1)}, bf16[16,1792]{1,0:T(8,128)(2,1)}, u32[]{:S(2)}) copy-start(bf16[16,1792]{1,0:T(8,128)(2,1)} %grads_ref.1) | copy-start | bytes 172036
  17.7 1.0 copy-start.1
  18.9 3.8 %collective-permute-start = (f32[256,512]{1,0:T(8,128)S(1)}, f32[256,512]{1,0:T(8,128)S(1)}, u32[]{:S(2)}, u32[]{:S(2)}) collective-permute-start(f32[256,512]{1,0:T(8,128)S(1)} %shard_map.47), channel_id=1, source_target_pairs={{0,1},{1,0},{2,3},{3,2},{4,5},{5,4},{6,7},{7,6},{8,9},{9,8},{10,11... | collective-permute-start | bytes 1572872 | tf_op jit(solution)/shard_map/ppermute | solution.py:128
  22.7 51.6 %copy-start = (bf16[1792,896]{1,0:T(8,128)(2,1)S(1)}, bf16[1792,896]{1,0:T(8,128)(2,1)}, u32[]{:S(2)}) copy-start(bf16[1792,896]{1,0:T(8,128)(2,1)} %basis_ref.7) | copy-start | bytes 9633796
  72.4 4.7 %collective-permute-start.1 = (bf16[16,16,2304]{2,1,0:T(8,128)(2,1)S(1)}, bf16[16,16,2304]{2,1,0:T(8,128)(2,1)S(1)}, u32[]{:S(2)}, u32[]{:S(2)}) collective-permute-start(bf16[16,16,2304]{2,1,0:T(8,128)(2,1)S(1)} %all_to_all.21.own_ref.packed_ref), channel_id=1, source_target_pairs={{0,1},{1,0},{2,3},{3,2},{4,5},{5,4},{6,7},{7,6},{8,9},{9,8},{10,11... | collective-permute-start | bytes 3538952 | tf_op jit(solution)/shard_map/ppermute | solution.py:133
  79.7 29.1 %all-to-all-start.2 = ((bf16[16,2,16,896]{3,2,1,0:T(8,128)(2,1)}), bf16[16,2,16,896]{3,2,1,0:T(8,128)(2,1)S(1)}, u32[]{:S(2)}, u32[]{:S(2)}) async-start(bf16[16,2,16,896]{3,2,1,0:T(8,128)(2,1)} %shard_map.50), calls=%async_computation.2 | async-start | bytes 1835008 | tf_op jit(solution)/shard_map/all_to_all | solution.py:35
  109.6 11.0 %all-to-all-start.3 = ((bf16[4,2,16,896]{3,2,1,0:T(8,128)(2,1)}), bf16[4,2,16,896]{3,2,1,0:T(8,128)(2,1)S(1)}, u32[]{:S(2)}, u32[]{:S(2)}) async-start(bf16[4,2,16,896]{3,2,1,0:T(8,128)(2,1)} %shard_map.52), calls=%async_computation.3 | async-start | bytes 458752 | tf_op jit(solution)/shard_map/all_to_all | solution.py:35
  116.7 19.7 %collective-permute-start.2 = (bf16[2,8,16,512]{3,2,1,0:T(8,128)(2,1)S(1)}, bf16[2,8,16,512]{3,2,1,0:T(8,128)(2,1)S(1)}, u32[]{:S(2)}, u32[]{:S(2)}) collective-permute-start(bf16[2,8,16,512]{3,2,1,0:T(8,128)(2,1)S(1)} %bitcast.3), channel_id=1, source_target_pairs={{0,16},{16,0},{1,17},{17,1},{2,18},{18,2},{3,19},{19,3},{4,20},{20... | collective-permute-start | bytes 786440 | tf_op jit(solution)/shard_map/ppermute | solution.py:168
